TPU v7x, 512 devices: a whole 4x8x8 slice. The times are simulated.
512 devices in a mesh: pipe: 16 (over z, x_lo), expert: 32 (over y, x_hi, core).
Axes of the slice: x: 4 (x_hi: 2, x_lo: 2; x = x_hi * 2 + x_lo), y: 8, z: 8, core: 2. Of those that a mesh axis runs over, the one named last changes fastest.
Arguments:
- fwd_tokens: bfloat16 [16, 1024, 7168], P('pipe', 'expert'), may hold values from -6 to 6
- fwd_routes: int32 [16, 4096, 4], P('pipe', 'expert'), may hold values from 0 to 31, all different within a row; in each aligned block of 128 rows (0 to 127, 128 to 255, ..., all dimensions but the last counted through in order) at most 24 rows name the same one
- fwd_mix: float32 [16, 4096, 4], P('pipe', 'expert'), may hold values from 0.2 to 1
- bwd_tokens: bfloat16 [16, 1024, 7168], P('pipe', 'expert'), may hold values from -6 to 6
- bwd_cotangent: bfloat16 [16, 1024, 7168], P('pipe', 'expert'), may hold values from -6 to 6
- bwd_routes: int32 [16, 4096, 4], P('pipe', 'expert'), may hold values from 0 to 31, all different within a row; in each aligned block of 128 rows (0 to 127, 128 to 255, ..., all dimensions but the last counted through in order) at most 24 rows name the same one
- bwd_mix: float32 [16, 4096, 4], P('pipe', 'expert'), may hold values from 0.2 to 1
- gate_up: bfloat16 [16, 32, 1792, 512], P('pipe', 'expert'), may hold values from -0.125 to 0.125
- down: bfloat16 [16, 32, 256, 1792], P('pipe', 'expert'), may hold values from -0.375 to 0.375
Outputs:
- next_forward: bfloat16 [16, 1024, 7168], P('pipe', 'expert')
- next_backward: bfloat16 [16, 1024, 7168], P('pipe', 'expert')
Inputs may be any that keep to these rules, and one draw needn't show every extreme that they name: `fwd_routes`: within the rows of one device (aligned blocks of 128 rows of a section) no expert is named by more than 24 rows, and a row names 4 different experts. `bwd_routes`: within the rows of one device (aligned blocks of 128 rows of a section) no expert is named by more than 24 rows, and a row names 4 different experts.
All inputs are finite; a program needn't handle non-finite values.
Results may differ from a plain program's by a relative error of at most 0.0057.
Values may be sent and summed in bfloat16 or wider, within the bound.
A program may use at most 64 MiB of HBM per device.

v0:
```python
import jax
import jax.numpy as jnp
from jax import lax
from jax.sharding import PartitionSpec as P


def shifted(value, axis, steps):
    count = lax.axis_size(axis)
    pairs = [(source, (source + steps) % count) for source in range(count)]
    return lax.ppermute(value, axis, pairs)


def block_places(routes, capacity, count_experts):
    flat_routes = routes.reshape(-1)
    onehot = (flat_routes[:, None] == jnp.arange(count_experts, dtype=jnp.int32)[None, :]).astype(
        jnp.int32
    )
    before = jnp.cumsum(onehot, axis=0) - onehot
    slot_index = jnp.sum(before * onehot, axis=1)
    return flat_routes * capacity + slot_index


def expert_forward(send_rows, w_gate_up, w_down):
    token_rows = send_rows.reshape(-1, send_rows.shape[-1])
    projected = jnp.dot(token_rows, w_gate_up, preferred_element_type=jnp.float32)
    width_hidden = w_down.shape[0]
    gate_value = projected[:, :width_hidden]
    up_value = projected[:, width_hidden:]
    hidden = (jax.nn.silu(gate_value) * up_value).astype(jnp.bfloat16)
    expert_out = jnp.dot(hidden, w_down, preferred_element_type=jnp.float32).astype(jnp.bfloat16)
    return expert_out.reshape(send_rows.shape)


def expert_backward(input_rows, grad_rows, w_gate_up, w_down):
    token_rows = input_rows.reshape(-1, input_rows.shape[-1])
    cotan_rows = grad_rows.reshape(-1, grad_rows.shape[-1])
    projected = jnp.dot(token_rows, w_gate_up, preferred_element_type=jnp.float32)
    width_hidden = w_down.shape[0]
    gate_value = projected[:, :width_hidden]
    up_value = projected[:, width_hidden:]
    sigmoid_gate = jax.nn.sigmoid(gate_value)
    d_hidden = jnp.dot(cotan_rows, w_down.T, preferred_element_type=jnp.float32)
    d_gate = d_hidden * up_value * sigmoid_gate * (1.0 + gate_value * (1.0 - sigmoid_gate))
    d_up = d_hidden * gate_value * sigmoid_gate
    d_both = jnp.concatenate([d_gate, d_up], axis=1).astype(jnp.bfloat16)
    d_rows = jnp.dot(d_both, w_gate_up.T, preferred_element_type=jnp.float32).astype(jnp.bfloat16)
    return d_rows.reshape(input_rows.shape)


def scatter_rows(source, target_rows, fanout, slot_total, sub_width):
    repeated = jnp.repeat(source.reshape(-1, sub_width), fanout, axis=0)
    send_rows = jnp.zeros((slot_total, sub_width), jnp.bfloat16).at[target_rows].set(repeated)
    return send_rows


def combine(returned, target_rows, mix_weights, sub_width):
    fanout = mix_weights.shape[-1]
    picked = (
        returned.reshape(-1, sub_width)[target_rows]
        .astype(jnp.float32)
        .reshape(-1, fanout, sub_width)
    )
    mixed = jnp.sum(mix_weights[:, :, None] * picked, axis=1)
    return mixed.astype(jnp.bfloat16)


def body(
    fwd_tokens, fwd_routes, fwd_mix, bwd_tokens, bwd_cotangent, bwd_routes, bwd_mix, gate_up, down
):
    w_gate_up = gate_up[0, 0]
    w_down = down[0, 0]
    experts = lax.axis_size("expert")
    sub_width = w_gate_up.shape[0]
    token_count = fwd_tokens.shape[1]
    model_width = fwd_tokens.shape[2]
    head_count = model_width // sub_width
    fanout = fwd_routes.shape[-1]
    capacity = 3 * token_count * head_count * fanout // (2 * experts)
    slot_total = experts * capacity
    target_fwd = block_places(fwd_routes[0], capacity, experts)
    target_bwd = block_places(bwd_routes[0], capacity, experts)
    send_fwd = scatter_rows(fwd_tokens[0], target_fwd, fanout, slot_total, sub_width).reshape(
        experts, capacity, sub_width
    )
    send_inp = scatter_rows(bwd_tokens[0], target_bwd, fanout, slot_total, sub_width).reshape(
        experts, capacity, sub_width
    )
    send_cot = scatter_rows(bwd_cotangent[0], target_bwd, fanout, slot_total, sub_width).reshape(
        experts, capacity, sub_width
    )
    out_fwd = expert_forward(
        lax.all_to_all(send_fwd, "expert", split_axis=0, concat_axis=0, tiled=True),
        w_gate_up,
        w_down,
    )
    returned_fwd = lax.all_to_all(out_fwd, "expert", split_axis=0, concat_axis=0, tiled=True)
    out_bwd = expert_backward(
        lax.all_to_all(send_inp, "expert", split_axis=0, concat_axis=0, tiled=True),
        lax.all_to_all(send_cot, "expert", split_axis=0, concat_axis=0, tiled=True),
        w_gate_up,
        w_down,
    )
    returned_bwd = lax.all_to_all(out_bwd, "expert", split_axis=0, concat_axis=0, tiled=True)
    forward_out = combine(returned_fwd, target_fwd, fwd_mix[0], sub_width).reshape(
        1, token_count, model_width
    )
    backward_out = combine(returned_bwd, target_bwd, bwd_mix[0], sub_width).reshape(
        1, token_count, model_width
    )
    next_forward = shifted(forward_out, "pipe", 1)
    next_backward = shifted(backward_out, "pipe", -1)
    return (next_forward, next_backward)


def solution(mesh):
    placed = (
        P("pipe", "expert", None),
        P("pipe", "expert", None),
        P("pipe", "expert", None),
        P("pipe", "expert", None),
        P("pipe", "expert", None),
        P("pipe", "expert", None),
        P("pipe", "expert", None),
        P("pipe", "expert", None, None),
        P("pipe", "expert", None, None),
    )
    return jax.shard_map(
        body,
        mesh=mesh,
        in_specs=placed,
        out_specs=(P("pipe", "expert", None), P("pipe", "expert", None)),
        check_vma=False,
    )
```

profile of v0, /device:TPU:12, one launch (start us, length us, event | category | flops | bytes accessed | tf_op | source)
XLA Modules:
  0.0 416.1 jit_solution(3082969335237511697)
XLA Ops:
  0.6 0.9 copy.24
  1.8 0.7 broadcast_multiply_fusion
  2.5 1.2 reduce-window.16
  3.7 0.2 slice_reduce_fusion
  4.1 1.3 reshape_squeeze.13
  5.5 1.7 broadcast_in_dim.8
  7.2 3.9 reshape.220
  11.2 6.1 %scatter_custom_fusion.2 = bf16[768,1792]{1,0:T(8,128)(2,1)} fusion(s32[512]{0:T(512)S(1)} %bitcast.76, bf16[512,1792]{1,0:T(8,128)(2,1)} %reshape.220, bf16[]{:T(256)} %constant.6.clone.1), kind=kCustom, calls=%fused_computation.14 | custom fusion | bytes 2753024 | tf_op jit(solution)/shard_map/scatter | solution.py:52
  17.4 10.3 %all-to-all-start.3 = ((bf16[32,24,1792]{2,1,0:T(8,128)(2,1)}), bf16[32,24,1792]{2,1,0:T(8,128)(2,1)}, u32[]{:S(2)}, u32[]{:S(2)}) async-start(bf16[32,24,1792]{2,1,0:T(8,128)(2,1)} %bitcast.73), calls=%async_computation.3 | async-start | bytes 5505024 | tf_op jit(solution)/shard_map/all_to_all | solution.py:98
  27.7 0.3 reshape_squeeze.12
  28.1 1.8 broadcast_in_dim.7
  29.8 4.0 reshape.212
  33.8 6.1 %scatter_custom_fusion.1 = bf16[768,1792]{1,0:T(8,128)(2,1)} fusion(s32[512]{0:T(512)S(1)} %bitcast.77, bf16[512,1792]{1,0:T(8,128)(2,1)} %reshape.212, bf16[]{:T(256)} %constant.6.clone.1), kind=kCustom, calls=%fused_computation.16 | custom fusion | bytes 2753024 | tf_op jit(solution)/shard_map/scatter | solution.py:52
  39.9 52.5 %all-to-all-done.3 = bf16[32,24,1792]{2,1,0:T(8,128)(2,1)} async-done(((bf16[32,24,1792]{2,1,0:T(8,128)(2,1)}), bf16[32,24,1792]{2,1,0:T(8,128)(2,1)}, u32[]{:S(2)}, u32[]{:S(2)}) %all-to-all-start.3) | async-done | bytes 2752544 | tf_op jit(solution)/shard_map/all_to_all | solution.py:98
  92.4 6.3 %all-to-all-start.2 = ((bf16[32,24,1792]{2,1,0:T(8,128)(2,1)}), bf16[32,24,1792]{2,1,0:T(8,128)(2,1)}, u32[]{:S(2)}, u32[]{:S(2)}) async-start(bf16[32,24,1792]{2,1,0:T(8,128)(2,1)} %bitcast.71), calls=%async_computation.2 | async-start | bytes 5505024 | tf_op jit(solution)/shard_map/all_to_all | solution.py:99
  98.7 0.1 copy.19
  99.1 1.2 reduce-window.14
  100.3 0.2 slice_reduce_fusion.1
  100.5 0.1 copy.18
  100.8 0.3 reshape_squeeze.11
  101.1 1.8 broadcast_in_dim.6
  102.9 4.0 reshape.204
  107.0 6.2 %scatter_custom_fusion = bf16[768,1792]{1,0:T(8,128)(2,1)} fusion(s32[512]{0:T(512)S(1)} %bitcast.79, bf16[512,1792]{1,0:T(8,128)(2,1)} %reshape.204, bf16[]{:T(256)} %constant.6.clone.1), kind=kCustom, calls=%fused_computation.18 | custom fusion | bytes 2753024 | tf_op jit(solution)/shard_map/scatter | solution.py:52
  113.2 50.2 %all-to-all-done.2 = bf16[32,24,1792]{2,1,0:T(8,128)(2,1)} async-done(((bf16[32,24,1792]{2,1,0:T(8,128)(2,1)}), bf16[32,24,1792]{2,1,0:T(8,128)(2,1)}, u32[]{:S(2)}, u32[]{:S(2)}) %all-to-all-start.2) | async-done | bytes 2752544 | tf_op jit(solution)/shard_map/all_to_all | solution.py:99
  163.4 5.9 %all-to-all-start = ((bf16[32,24,1792]{2,1,0:T(8,128)(2,1)}), bf16[32,24,1792]{2,1,0:T(8,128)(2,1)}, u32[]{:S(2)}, u32[]{:S(2)}) async-start(bf16[32,24,1792]{2,1,0:T(8,128)(2,1)} %bitcast.72), calls=%async_computation | async-start | bytes 5505024 | tf_op jit(solution)/shard_map/all_to_all | solution.py:92
  169.3 3.4 fusion.1
  172.8 2.8 fusion.16
  175.6 3.2 convolution_convert_fusion
  178.8 55.1 %all-to-all-done = bf16[32,24,1792]{2,1,0:T(8,128)(2,1)} async-done(((bf16[32,24,1792]{2,1,0:T(8,128)(2,1)}), bf16[32,24,1792]{2,1,0:T(8,128)(2,1)}, u32[]{:S(2)}, u32[]{:S(2)}) %all-to-all-start) | async-done | bytes 2752544 | tf_op jit(solution)/shard_map/all_to_all | solution.py:92
  233.9 5.9 %all-to-all-start.4 = ((bf16[32,24,1792]{2,1,0:T(8,128)(2,1)}), bf16[32,24,1792]{2,1,0:T(8,128)(2,1)}, u32[]{:S(2)}, u32[]{:S(2)}) async-start(bf16[32,24,1792]{2,1,0:T(8,128)(2,1)} %bitcast.75), calls=%async_computation.4 | async-start | bytes 5505024 | tf_op jit(solution)/shard_map/all_to_all | solution.py:103
  239.9 3.3 fusion.3
  243.2 2.6 convolution_convert_fusion.1
  245.8 58.7 %all-to-all-done.4 = bf16[32,24,1792]{2,1,0:T(8,128)(2,1)} async-done(((bf16[32,24,1792]{2,1,0:T(8,128)(2,1)}), bf16[32,24,1792]{2,1,0:T(8,128)(2,1)}, u32[]{:S(2)}, u32[]{:S(2)}) %all-to-all-start.4) | async-done | bytes 2752544 | tf_op jit(solution)/shard_map/all_to_all | solution.py:103
  304.5 6.1 %all-to-all-start.1 = ((bf16[32,24,1792]{2,1,0:T(8,128)(2,1)}), bf16[32,24,1792]{2,1,0:T(8,128)(2,1)}, u32[]{:S(2)}, u32[]{:S(2)}) async-start(bf16[32,24,1792]{2,1,0:T(8,128)(2,1)} %bitcast.74), calls=%async_computation.1 | async-start | bytes 5505024 | tf_op jit(solution)/shard_map/all_to_all | solution.py:96
  310.8 6.9 %gather_fusion.1 = bf16[512,1792]{1,0:T(8,128)(2,1)} fusion(bf16[768,1792]{1,0:T(8,128)(2,1)} %bitcast.19, s32[1024]{0:T(1024)S(1)} %pad_clamp_fusion), kind=kCustom, calls=%fused_computation.1 | custom fusion | bytes 3672064 | tf_op jit(solution)/shard_map/gather | solution.py:59
  317.7 4.5 %reshape.183 = f32[128,4,1792]{2,1,0:T(4,128)} reshape(bf16[512,1792]{1,0:T(8,128)(2,1)} %gather_fusion.1) | data formatting | bytes 5505024 | tf_op jit(solution)/shard_map/convert_element_type | solution.py:60
  322.2 4.7 %multiply_reduce_fusion = bf16[128,1792]{1,0:T(8,128)(2,1)S(1)} fusion(f32[128,4,1792]{2,1,0:T(4,128)} %reshape.183, f32[128,4]{1,0:T(8,128)S(1)} %copy.22), kind=kLoop, calls=%fused_computation.5 | loop fusion | flops 1605632 | bytes 4130816 | tf_op jit(solution)/shard_map/reduce_sum | solution.py:63
  326.9 0.3 convert_element_type.78
  327.2 11.4 %collective-permute-start.1 = (bf16[1,32,7168]{2,1,0:T(8,128)(2,1)S(1)}, bf16[1,32,7168]{2,1,0:T(8,128)(2,1)S(1)}, u32[]{:S(2)}, u32[]{:S(2)}) collective-permute-start(bf16[1,32,7168]{2,1,0:T(8,128)(2,1)S(1)} %convert_element_type.78), channel_id=1, source_target_pairs={{0,480},{32,0},{64,32},{96,64},{128,96},{160,128},{192,160},{224,1... | collective-permute-start | bytes 1376264 | tf_op jit(solution)/shard_map/ppermute | solution.py:10
  338.6 36.6 %all-to-all-done.1 = bf16[32,24,1792]{2,1,0:T(8,128)(2,1)} async-done(((bf16[32,24,1792]{2,1,0:T(8,128)(2,1)}), bf16[32,24,1792]{2,1,0:T(8,128)(2,1)}, u32[]{:S(2)}, u32[]{:S(2)}) %all-to-all-start.1) | async-done | bytes 2752544 | tf_op jit(solution)/shard_map/all_to_all | solution.py:96
  375.2 6.9 %gather_fusion = bf16[512,1792]{1,0:T(8,128)(2,1)} fusion(bf16[768,1792]{1,0:T(8,128)(2,1)} %bitcast.9, s32[1024]{0:T(1024)S(1)} %pad_clamp_fusion.1), kind=kCustom, calls=%fused_computation | custom fusion | bytes 3672064 | tf_op jit(solution)/shard_map/gather | solution.py:59
  382.1 4.5 %reshape.182 = f32[128,4,1792]{2,1,0:T(4,128)} reshape(bf16[512,1792]{1,0:T(8,128)(2,1)} %gather_fusion) | data formatting | bytes 5505024 | tf_op jit(solution)/shard_map/convert_element_type | solution.py:60
  386.5 4.7 %multiply_reduce_fusion.1 = bf16[128,1792]{1,0:T(8,128)(2,1)S(1)} fusion(f32[128,4,1792]{2,1,0:T(4,128)} %reshape.182, f32[128,4]{1,0:T(8,128)S(1)} %copy.17), kind=kLoop, calls=%fused_computation.6 | loop fusion | flops 1605632 | bytes 4130816 | tf_op jit(solution)/shard_map/reduce_sum | solution.py:63
  391.2 1.1 convert_element_type.71
  392.3 2.9 collective-permute-start
  395.2 19.3 %collective-permute-done = bf16[1,32,7168]{2,1,0:T(8,128)(2,1)S(1)} collective-permute-done((bf16[1,32,7168]{2,1,0:T(8,128)(2,1)}, bf16[1,32,7168]{2,1,0:T(8,128)(2,1)S(1)}, u32[]{:S(2)}, u32[]{:S(2)}) %collective-permute-start) | collective-permute-done | bytes 458784 | tf_op jit(solution)/shard_map/ppermute | solution.py:10
  414.6 0.8 copy.39
  415.3 0.8 copy.40
  (37 shorter events, 1.3 us)
Async XLA Ops:
  0.6 168.7 %copy-start = (bf16[1,1,1792,512]{3,2,1,0:T(8,128)(2,1)S(1)}, bf16[1,1,1792,512]{3,2,1,0:T(8,128)(2,1)}, u32[]{:S(2)}) copy-start(bf16[1,1,1792,512]{3,2,1,0:T(8,128)(2,1)} %param.16) | copy-start | bytes 5505028
  17.4 10.3 %copy-start.1 = (bf16[1,32,7168]{2,1,0:T(8,128)(2,1)S(1)}, bf16[1,32,7168]{2,1,0:T(8,128)(2,1)}, u32[]{:S(2)}) copy-start(bf16[1,32,7168]{2,1,0:T(8,128)(2,1)} %param.13) | copy-start | bytes 1376260
  17.4 75.0 %all-to-all-start.3 = ((bf16[32,24,1792]{2,1,0:T(8,128)(2,1)}), bf16[32,24,1792]{2,1,0:T(8,128)(2,1)}, u32[]{:S(2)}, u32[]{:S(2)}) async-start(bf16[32,24,1792]{2,1,0:T(8,128)(2,1)} %bitcast.73), calls=%async_computation.3 | async-start | bytes 5505024 | tf_op jit(solution)/shard_map/all_to_all | solution.py:98
  92.4 6.3 %copy-start.3 = (s32[1,128,4]{1,2,0:T(4,128)S(1)}, s32[1,128,4]{1,2,0:T(4,128)}, u32[]{:S(2)}) copy-start(s32[1,128,4]{1,2,0:T(4,128)} %param.10) | copy-start | bytes 6148
  92.4 8.3 %copy-start.2 = (bf16[1,32,7168]{2,1,0:T(8,128)(2,1)S(1)}, bf16[1,32,7168]{2,1,0:T(8,128)(2,1)}, u32[]{:S(2)}) copy-start(bf16[1,32,7168]{2,1,0:T(8,128)(2,1)} %param.9) | copy-start | bytes 1376260
  92.4 70.9 %all-to-all-start.2 = ((bf16[32,24,1792]{2,1,0:T(8,128)(2,1)}), bf16[32,24,1792]{2,1,0:T(8,128)(2,1)}, u32[]{:S(2)}, u32[]{:S(2)}) async-start(bf16[32,24,1792]{2,1,0:T(8,128)(2,1)} %bitcast.71), calls=%async_computation.2 | async-start | bytes 5505024 | tf_op jit(solution)/shard_map/all_to_all | solution.py:99
  163.4 70.6 %all-to-all-start = ((bf16[32,24,1792]{2,1,0:T(8,128)(2,1)}), bf16[32,24,1792]{2,1,0:T(8,128)(2,1)}, u32[]{:S(2)}, u32[]{:S(2)}) async-start(bf16[32,24,1792]{2,1,0:T(8,128)(2,1)} %bitcast.72), calls=%async_computation | async-start | bytes 5505024 | tf_op jit(solution)/shard_map/all_to_all | solution.py:92
  169.3 3.5 copy-start.6
  233.9 70.6 %all-to-all-start.4 = ((bf16[32,24,1792]{2,1,0:T(8,128)(2,1)}), bf16[32,24,1792]{2,1,0:T(8,128)(2,1)}, u32[]{:S(2)}, u32[]{:S(2)}) async-start(bf16[32,24,1792]{2,1,0:T(8,128)(2,1)} %bitcast.75), calls=%async_computation.4 | async-start | bytes 5505024 | tf_op jit(solution)/shard_map/all_to_all | solution.py:103
  304.5 6.1 %copy-start.4 = (f32[1,128,4]{1,2,0:T(4,128)S(1)}, f32[1,128,4]{1,2,0:T(4,128)}, u32[]{:S(2)}) copy-start(f32[1,128,4]{1,2,0:T(4,128)} %param.15) | copy-start | bytes 6148
  304.5 6.2 %copy-start.5 = (f32[1,128,4]{1,2,0:T(4,128)S(1)}, f32[1,128,4]{1,2,0:T(4,128)}, u32[]{:S(2)}) copy-start(f32[1,128,4]{1,2,0:T(4,128)} %param.11) | copy-start | bytes 6148
  304.5 70.7 %all-to-all-start.1 = ((bf16[32,24,1792]{2,1,0:T(8,128)(2,1)}), bf16[32,24,1792]{2,1,0:T(8,128)(2,1)}, u32[]{:S(2)}, u32[]{:S(2)}) async-start(bf16[32,24,1792]{2,1,0:T(8,128)(2,1)} %bitcast.74), calls=%async_computation.1 | async-start | bytes 5505024 | tf_op jit(solution)/shard_map/all_to_all | solution.py:96
  327.2 68.0 %collective-permute-start.1 = (bf16[1,32,7168]{2,1,0:T(8,128)(2,1)S(1)}, bf16[1,32,7168]{2,1,0:T(8,128)(2,1)S(1)}, u32[]{:S(2)}, u32[]{:S(2)}) collective-permute-start(bf16[1,32,7168]{2,1,0:T(8,128)(2,1)S(1)} %convert_element_type.78), channel_id=1, source_target_pairs={{0,480},{32,0},{64,32},{96,64},{128,96},{160,128},{192,160},{224,1... | collective-permute-start | bytes 1376264 | tf_op jit(solution)/shard_map/ppermute | solution.py:10
  392.3 22.3 %collective-permute-start = (bf16[1,32,7168]{2,1,0:T(8,128)(2,1)}, bf16[1,32,7168]{2,1,0:T(8,128)(2,1)S(1)}, u32[]{:S(2)}, u32[]{:S(2)}) collective-permute-start(bf16[1,32,7168]{2,1,0:T(8,128)(2,1)} %convert_element_type.71), channel_id=1, source_target_pairs={{0,32},{32,64},{64,96},{96,128},{128,160},{160,192},{192,224},{224... | collective-permute-start | bytes 1376264 | tf_op jit(solution)/shard_map/ppermute | solution.py:10
where the time goes:
time: 417 us; the launch traced here: 416 us
  waiting for transfers between devices  272 us (65%)
  local copies, waits for them, and re-layouts  65.9 us (16%)
  starting transfers between devices  48.8 us (12%)
  matrix products  15.4 us (4%)
  other arithmetic  12.7 us (3%)
    all_to_all x1, waiting for transfers between devices, body(): lax.all_to_all(out_bwd, 'expert', split_axis=0, concat_axis=0, tiled=True)  58.7 us
    all_to_all x1, waiting for transfers between devices, body(): lax.all_to_all(send_fwd, 'expert', split_axis=0, concat_axis=0, tiled=True)  55.1 us
    all_to_all x1, waiting for transfers between devices, body(): lax.all_to_all(send_inp, 'expert', split_axis=0, concat_axis=0, tiled=True)  52.5 us
    all_to_all x1, waiting for transfers between devices, body(): lax.all_to_all(send_cot, 'expert', split_axis=0, concat_axis=0, tiled=True)  50.2 us
    all_to_all x1, waiting for transfers between devices, body(): lax.all_to_all(out_fwd, 'expert', split_axis=0, concat_axis=0, tiled=True)  36.6 us
    ppermute x2, waiting for transfers between devices, shifted(): return lax.ppermute(value, axis, pairs)  19.3 us
    scatter x3, local copies, waits for them, and re-layouts, scatter_rows(): jnp.zeros((slot_total, sub_width), jnp.bfloat16).at[target_rows]  18.5 us
    ppermute x2, starting transfers between devices, shifted(): return lax.ppermute(value, axis, pairs)  14.3 us
  transfers between devices with their start and end apart: 7, of which 6 were waited for; matrix products, arithmetic and copies ran while one was open for 18% of the time, Pallas kernels for 0%

commit v1 on v0

v1 whole, which is shorter than its diff:
```python
import functools

import jax
import jax.numpy as jnp
from jax import lax
from jax.experimental import pallas as pl
from jax.experimental.pallas import tpu as pltpu
from jax.sharding import PartitionSpec as P

MESH = pl.DeviceIdType.MESH
RING = 8
PLANE = 4
TOP = 4
ROWS = 128
HALF = ROWS // 2
PART = 32
WIDTH = 1792
HID = 256
PIECES = 6
FWD, SAVED, COT = 0, 1, 2
PLUS, MINUS = 0, 1

OWN, FAR = 0, 1


def place(distance, way):
    return 2 * distance + way


STEP_ROW = {1: 0, 2: HALF, 3: HALF + ROWS, 4: HALF + 2 * ROWS}


def dot(a, b):
    return jnp.dot(a, b, preferred_element_type=jnp.float32)


def dot_t(a, b):
    return lax.dot_general(a, b, (((1,), (1,)), ((), ())), preferred_element_type=jnp.float32)


def kernel(
    fwd_tokens, fwd_routes, fwd_mix, saved, cotangent, bwd_routes, bwd_mix, gate_up, down,
    out_fwd, out_bwd,
    x, gu, dn, part, got, begun, done, hid, both, wt, wr, wc,
    load_sem, gs, gr, ss, sr, os_, or_, xs, xr, cs, cr, rs, rr, ws, wrs,
):
    ex = lax.axis_index("expert")
    pi = lax.axis_index("pipe")
    sections = 16
    y = ex // PLANE
    seat = ex % PLANE
    xh = seat // 2
    core = seat % 2

    def ring(delta):
        return {"pipe": pi, "expert": ((y + delta) % RING) * PLANE + seat}

    mate_seat = (1 - xh) * 2 + core
    mate = {"pipe": pi, "expert": y * PLANE + mate_seat}
    twin = {"pipe": pi, "expert": y * PLANE + xh * 2 + (1 - core)}
    later = {"pipe": (pi + 1) % sections, "expert": ex}
    earlier = {"pipe": (pi + sections - 1) % sections, "expert": ex}
    side = {PLUS: ring(1), MINUS: ring(RING - 1)}

    def load(index, source, target):
        copy = pltpu.make_async_copy(source, target, load_sem.at[index])
        copy.start()
        return copy

    token_loads = []
    for a, source in enumerate((fwd_tokens, saved, cotangent)):
        token_loads.append([
            load(4 * a + h, source.at[0, :, pl.ds(h * WIDTH, WIDTH)], x.at[a, pl.ds(PART * h, PART), :])
            for h in range(4)
        ])
    weight_loads = [load(12, gate_up.at[0, 0], gu.at[seat]), load(13, down.at[0, 0], dn.at[seat])]

    barrier = pltpu.get_barrier_semaphore()
    met = [ring(d) for d in range(1, RING)] + [mate, twin, later, earlier]
    for device in met:
        pl.semaphore_signal(barrier, inc=1, device_id=device, device_id_type=MESH)
    pl.semaphore_wait(barrier, len(met))

    def remote(source, target, send, receive, device):
        return pltpu.make_async_remote_copy(
            src_ref=source, dst_ref=target, send_sem=send, recv_sem=receive,
            device_id=device, device_id_type=MESH,
        )

    def gather(a, way, hop):
        index = (a * 2 + way) * 4 + hop - 1
        if hop == 4:
            low = HALF * way
            source = x.at[a, pl.ds(place(3, way) * ROWS + low, HALF), :]
            target = x.at[a, pl.ds(FAR * ROWS + low, HALF), :]
        else:
            source = x.at[a, pl.ds((place(hop - 1, way) if hop > 1 else OWN) * ROWS, ROWS), :]
            target = x.at[a, pl.ds(place(hop, way) * ROWS, ROWS), :]
        return remote(source, target, gs.at[index], gr.at[index], side[way])

    def gather_start(a, hop):
        for way in (PLUS, MINUS):
            gather(a, way, hop).start()

    def gather_wait(a, hop):
        for way in (PLUS, MINUS):
            gather(a, way, hop).wait_recv()

    def relay(a, hop):
        gather_wait(a, hop)
        gather_start(a, hop + 1)

    for a in (FWD, SAVED, COT):
        for copy in token_loads[a]:
            copy.wait()
        gather_start(a, 1)

    def piece(owner, i):
        if i < 4:
            return gu.at[owner, pl.ds(448 * i, 448), :]
        return dn.at[owner, pl.ds(128 * (i - 4), 128), :]

    for copy in weight_loads:
        copy.wait()
    to_mate = [remote(piece(seat, i), piece(seat, i), xs.at[i], xr.at[i], mate) for i in range(PIECES)]
    to_twin = [remote(piece(seat, i), piece(seat, i), cs.at[i], cr.at[i], twin) for i in range(PIECES)]
    passed = [
        remote(piece(mate_seat, i), piece(mate_seat, i), rs.at[i], rr.at[i], twin) for i in range(PIECES)
    ]
    for i in range(PIECES):
        to_mate[i].start()
    for i in range(PIECES):
        to_twin[i].start()

    lane = lax.broadcasted_iota(jnp.int32, (ROWS, ROWS), 1)
    row = lax.broadcasted_iota(jnp.int32, (ROWS, ROWS), 0)
    order = (row == (lane % PART) * 4 + lane // PART).astype(jnp.float32)

    def by_expert(routes, mix):
        chosen = routes[0]
        weight = mix[0]
        spread = jnp.zeros((ROWS, ROWS), jnp.float32)
        for k in range(TOP):
            spread = spread + jnp.where(chosen[:, k : k + 1] == lane, weight[:, k : k + 1], 0.0)
        return jnp.dot(spread.T, order, precision=lax.Precision.HIGHEST, preferred_element_type=jnp.float32)

    for a, (routes, mix) in enumerate(((fwd_routes, fwd_mix), (bwd_routes, bwd_mix))):
        table = by_expert(routes, mix)
        for at in range(RING):
            wt[at, pl.ds(4 * a, 4), :] = table[4 * at : 4 * at + 4, :]

    def source_place(delta):
        if delta == 4:
            return FAR
        return place(delta, PLUS) if delta < 4 else place(RING - delta, MINUS)

    mixes = [
        remote(wt.at[(y + d) % RING], wr.at[source_place(d)], ws.at[d - 1], wrs.at[d - 1], ring(d))
        for d in range(1, RING)
    ]
    for copy in mixes:
        copy.start()
    wr[OWN] = wt[y]

    relay(FWD, 1)
    relay(SAVED, 1)
    relay(COT, 1)
    for copy in mixes:
        copy.wait_recv()
    for s in range(RING):
        wc[pl.ds(s * ROWS, ROWS), :] = wr[s].T
    relay(FWD, 2)
    relay(SAVED, 2)
    relay(COT, 2)
    for i in range(PIECES):
        to_mate[i].wait_recv()
        passed[i].start()
    for i in range(PIECES):
        to_twin[i].wait_recv()
    for i in range(PIECES):
        passed[i].wait_recv()

    def compute_fwd(pair):
        rows = pl.ds(pair * 2 * ROWS, 2 * ROWS)
        for e in range(PLANE):
            projected = dot(x[FWD, rows, :], gu[e])
            gate, up = projected[:, :HID], projected[:, HID:]
            hidden = gate * jax.nn.sigmoid(gate) * up * wc[rows, e : e + 1]
            hid[:, e * HID : (e + 1) * HID] = hidden.astype(jnp.bfloat16)
        for n in range(WIDTH // 256):
            cols = slice(n * 256, (n + 1) * 256)
            total = dot(hid[:, :HID], dn[0, :, cols])
            for e in range(1, PLANE):
                total = total + dot(hid[:, e * HID : (e + 1) * HID], dn[e, :, cols])
            part[0, rows, cols] = total

    def compute_bwd(pair):
        rows = pl.ds(pair * 2 * ROWS, 2 * ROWS)
        for e in range(PLANE):
            projected = dot(x[SAVED, rows, :], gu[e])
            gate, up = projected[:, :HID], projected[:, HID:]
            d_hidden = dot_t(x[COT, rows, :], dn[e]) * wc[rows, 4 + e : 5 + e]
            sig = jax.nn.sigmoid(gate)
            d_gate = d_hidden * up * sig * (1.0 + gate * (1.0 - sig))
            d_up = d_hidden * gate * sig
            both[:, e * 2 * HID : e * 2 * HID + HID] = d_gate.astype(jnp.bfloat16)
            both[:, e * 2 * HID + HID : (e + 1) * 2 * HID] = d_up.astype(jnp.bfloat16)
        for n in range(WIDTH // 256):
            cols = slice(n * 256, (n + 1) * 256)
            total = dot_t(both[:, : 2 * HID], gu[0, cols, :])
            for e in range(1, PLANE):
                total = total + dot_t(both[:, e * 2 * HID : (e + 1) * 2 * HID], gu[e, cols, :])
            part[1, rows, cols] = total

    def back_copy(m, way, step, h):
        index = ((m * 2 + way) * 4 + step - 1) * 4 + h
        here = HALF if step == 1 else ROWS
        low = PART * h - (HALF * way if step == 1 else 0)
        fresh = step == 1 or (step == 2 and h // 2 != way)
        if fresh:
            at = (0 if step == 1 else HALF) + PART * (h % 2)
            source = begun.at[m, way, pl.ds(at, PART), :]
        else:
            before = PART * h - (HALF * way if step == 2 else 0)
            source = got.at[m, way, pl.ds(STEP_ROW[step - 1] + before, PART), :]
        target = got.at[m, way, pl.ds(STEP_ROW[step] + low, PART), :]
        return remote(source, target, ss.at[index], sr.at[index], side[1 - way])

    def block_at(step, way):
        return FAR if step == 1 else place(5 - step, way)

    def back_fresh(m, way, step, h):
        at = (0 if step == 1 else HALF) + PART * (h % 2)
        begun[m, way, pl.ds(at, PART), :] = part[
            m, pl.ds(block_at(step, way) * ROWS + PART * h, PART), :
        ].astype(jnp.bfloat16)
        back_copy(m, way, step, h).start()

    def back_begin(m):
        for h in range(2):
            for way in (PLUS, MINUS):
                back_fresh(m, way, 1, h + 2 * way)

    def back_begin_second(m):
        for h in range(2):
            for way in (PLUS, MINUS):
                back_fresh(m, way, 2, h + 2 * (1 - way))

    def back_add(m, way, step, h):
        back_copy(m, way, step - 1, h).wait_recv()
        before = PART * h - (HALF * way if step == 2 else 0)
        rows = pl.ds(STEP_ROW[step - 1] + before, PART)
        mine = part[m, pl.ds(block_at(step, way) * ROWS + PART * h, PART), :]
        got[m, way, rows, :] = (got[m, way, rows, :].astype(jnp.float32) + mine).astype(jnp.bfloat16)
        back_copy(m, way, step, h).start()

    def back_step(m, step):
        for h in range(2 if step == 2 else 4):
            for way in (PLUS, MINUS):
                if step == 2:
                    back_add(m, way, step, h + 2 * way)
                elif step == 3:
                    back_add(m, way, step, (h + 2 * (1 - way)) % 4)
                else:
                    back_add(m, way, step, (h + 2 * (1 - way)) % 4)

    outs = [
        [
            remote(
                done.at[m, pl.ds(PART * h, PART), :],
                (out_fwd, out_bwd)[m].at[0, :, pl.ds(h * WIDTH, WIDTH)],
                os_.at[m * 4 + h], or_.at[m * 4 + h], (later, earlier)[m],
            )
            for h in range(4)
        ]
        for m in range(2)
    ]

    def finish(m):
        for h in range(4):
            for way in (PLUS, MINUS):
                back_copy(m, way, 4, h).wait_recv()
            rows = pl.ds(PART * h, PART)
            last = pl.ds(STEP_ROW[4] + PART * h, PART)
            total = part[m, pl.ds(OWN * ROWS + PART * h, PART), :]
            for way in (PLUS, MINUS):
                total = total + got[m, way, last, :].astype(jnp.float32)
            done[m, rows, :] = total.astype(jnp.bfloat16)
            outs[m][h].start()

    compute_fwd(1)
    relay(FWD, 3)
    compute_fwd(2)
    relay(SAVED, 3)
    compute_fwd(3)
    compute_bwd(1)
    relay(COT, 3)
    gather_wait(FWD, 4)
    compute_fwd(0)
    back_begin(0)
    back_begin_second(0)
    compute_bwd(2)
    back_step(0, 2)
    compute_bwd(3)
    back_step(0, 3)
    gather_wait(SAVED, 4)
    gather_wait(COT, 4)
    compute_bwd(0)
    back_begin(1)
    back_begin_second(1)
    back_step(0, 4)
    back_step(1, 2)
    finish(0)
    back_step(1, 3)
    back_step(1, 4)
    finish(1)

    for a in (FWD, SAVED, COT):
        for hop in range(1, 5):
            for way in (PLUS, MINUS):
                gather(a, way, hop).wait_send()
    for i in range(PIECES):
        to_mate[i].wait_send()
        to_twin[i].wait_send()
        passed[i].wait_send()
    for copy in mixes:
        copy.wait_send()
    for m in range(2):
        for way in (PLUS, MINUS):
            for step in range(1, 5):
                for h in range(2) if step == 1 else range(4):
                    back_copy(m, way, step, h + 2 * way if step == 1 else h).wait_send()
        for h in range(4):
            outs[m][h].wait_send()
            outs[m][h].wait_recv()


def body(*operands):
    hbm = pl.BlockSpec(memory_space=pl.ANY)
    vmem = pl.BlockSpec(memory_space=pltpu.VMEM)
    out = jax.ShapeDtypeStruct(operands[0].shape, jnp.bfloat16)
    dma = pltpu.SemaphoreType.DMA
    bf16, f32 = jnp.bfloat16, jnp.float32
    return pl.pallas_call(
        kernel,
        out_shape=(out, out),
        in_specs=[hbm, vmem, vmem, hbm, hbm, vmem, vmem, hbm, hbm],
        out_specs=(hbm, hbm),
        scratch_shapes=[
            pltpu.VMEM((3, RING * ROWS, WIDTH), bf16),
            pltpu.VMEM((PLANE, WIDTH, 2 * HID), bf16),
            pltpu.VMEM((PLANE, HID, WIDTH), bf16),
            pltpu.VMEM((2, RING * ROWS, WIDTH), f32),
            pltpu.VMEM((2, 2, HALF + 3 * ROWS, WIDTH), bf16),
            pltpu.VMEM((2, 2, ROWS, WIDTH), bf16),
            pltpu.VMEM((2, ROWS, WIDTH), bf16),
            pltpu.VMEM((2 * ROWS, PLANE * HID), bf16),
            pltpu.VMEM((2 * ROWS, PLANE * 2 * HID), bf16),
            pltpu.VMEM((RING, 8, ROWS), f32),
            pltpu.VMEM((RING, 8, ROWS), f32),
            pltpu.VMEM((RING * ROWS, 8), f32),
            dma((14,)),
            dma((24,)), dma((24,)),
            dma((64,)), dma((64,)),
            dma((8,)), dma((8,)),
            dma((PIECES,)), dma((PIECES,)),
            dma((PIECES,)), dma((PIECES,)),
            dma((PIECES,)), dma((PIECES,)),
            dma((RING - 1,)), dma((RING - 1,)),
        ],
        name="moe_relay",
        compiler_params=pltpu.CompilerParams(
            collective_id=0, has_side_effects=True, vmem_limit_bytes=60 * 1024 * 1024
        ),
    )(*operands)


def solution(mesh):
    spec3 = P("pipe", "expert", None)
    spec4 = P("pipe", "expert", None, None)
    return jax.shard_map(
        body,
        mesh=mesh,
        in_specs=(spec3,) * 7 + (spec4,) * 2,
        out_specs=(spec3, spec3),
        check_vma=False,
    )
```

time: 417 us -> 208 us (0.50)
  the two profiles are of different devices: /device:TPU:12 before, /device:TPU:24 now
where the time goes in v1:
time: 208 us
  Pallas kernels  198 us (95%)
  local copies, waits for them, and re-layouts  9.3 us (4%)
    pallas_call x1, Pallas kernels, body(): pl.pallas_call(kernel, out_shape=(out, out), in_specs=[hbm, vmem, vmem, h...  198 us
    unnamed x6, local copies, waits for them, and re-layouts  9.3 us

profile of v1, /device:TPU:24, one launch (start us, length us, event | category | flops | bytes accessed | tf_op | source)
XLA Modules:
  0.0 207.8 jit_solution(3701118103639947662)
XLA Ops:
  0.6 1.4 copy.11.fwd_routes
  2.0 1.4 copy.12.fwd_mix
  3.5 1.4 copy.13.bwd_routes
  4.9 1.4 copy.14.bwd_mix
  6.3 197.9 %moe_relay.1 = (bf16[1,32,7168]{2,1,0:T(8,128)(2,1)}, bf16[1,32,7168]{2,1,0:T(8,128)(2,1)}) custom-call(bf16[1,32,7168]{2,1,0:T(8,128)(2,1)} %fwd_tokens.1, s32[1,128,4]{2,1,0:T(8,128)} %copy.11.fwd_routes, f32[1,128,4]{2,1,0:T(8,128)} %copy.12.fwd_mix, bf16[1,32,7168]{2,1,0:T(8,128)(2,1)} %saved.1, bf16[1,32,7168]{2,1,0:T(8,128)(2,1)} %cotangent.1, ...), custom_call_target="tpu_custom_call" | custom-call | tf_op jit(solution)/shard_map/moe_relay/pallas_call | solution.py:344
  204.2 1.8 copy.17
  206.0 1.8 copy.18

commit v2 on v1

v2 whole, which is shorter than its diff:
```python
import functools

import jax
import jax.numpy as jnp
from jax import lax
from jax.experimental import pallas as pl
from jax.experimental.pallas import tpu as pltpu
from jax.sharding import PartitionSpec as P

MESH = pl.DeviceIdType.MESH
RING = 8
PLANE = 4
TOP = 4
ROWS = 128
PART = 32
HOP_ROWS = {1: 128, 2: 128, 3: 112, 4: 48}
LIMIT3, LIMIT4 = float(HOP_ROWS[3]), float(HOP_ROWS[4])
WIDTH = 1792
HID = 256
PIECES = 6
FWD, SAVED, COT = 0, 1, 2
PLUS, MINUS = 0, 1

OWN, FAR = 0, 1


def place(distance, way):
    return 2 * distance + way


BACK_ROWS = {1: 48, 2: 112, 3: 128, 4: 128}
STEP_ROW = {1: 0, 2: 112, 3: 240, 4: 368}
GOT_ROWS = 496
COLS = [(0, 512), (512, 512), (1024, 384), (1408, 384)]


def dot(a, b):
    return jnp.dot(a, b, preferred_element_type=jnp.float32)


def dot_t(a, b):
    return lax.dot_general(a, b, (((1,), (1,)), ((), ())), preferred_element_type=jnp.float32)


def kernel(
    fwd_tokens, fwd_routes, fwd_mix, saved, cotangent, bwd_routes, bwd_mix, gate_up, down,
    out_fwd, out_bwd,
    x, xp, gu, dn, part, got, begun, done, hid, both, perm, back, wt, wr, wc,
    load_sem, gs, gr, ss, sr, os_, or_, xs, xr, cs, cr, rs, rr, ws, wrs,
):
    ex = lax.axis_index("expert")
    pi = lax.axis_index("pipe")
    sections = 16
    y = ex // PLANE
    seat = ex % PLANE
    xh = seat // 2
    core = seat % 2

    def ring(delta):
        return {"pipe": pi, "expert": ((y + delta) % RING) * PLANE + seat}

    mate_seat = (1 - xh) * 2 + core
    mate = {"pipe": pi, "expert": y * PLANE + mate_seat}
    twin = {"pipe": pi, "expert": y * PLANE + xh * 2 + (1 - core)}
    later = {"pipe": (pi + 1) % sections, "expert": ex}
    earlier = {"pipe": (pi + sections - 1) % sections, "expert": ex}
    side = {PLUS: ring(1), MINUS: ring(RING - 1)}

    def load(index, source, target):
        copy = pltpu.make_async_copy(source, target, load_sem.at[index])
        copy.start()
        return copy

    token_loads = []
    for a, source in enumerate((fwd_tokens, saved, cotangent)):
        token_loads.append([
            load(4 * a + h, source.at[0, :, pl.ds(h * WIDTH, WIDTH)], x.at[a, pl.ds(PART * h, PART), :])
            for h in range(4)
        ])
    weight_loads = [load(12, gate_up.at[0, 0], gu.at[seat]), load(13, down.at[0, 0], dn.at[seat])]

    barrier = pltpu.get_barrier_semaphore()
    met = [ring(d) for d in range(1, RING)] + [mate, twin, later, earlier]
    for device in met:
        pl.semaphore_signal(barrier, inc=1, device_id=device, device_id_type=MESH)

    lane = lax.broadcasted_iota(jnp.int32, (ROWS, ROWS), 1)
    row = lax.broadcasted_iota(jnp.int32, (ROWS, ROWS), 0)
    order = (row == (lane % PART) * 4 + lane // PART).astype(jnp.float32)
    before = (row < lane).astype(jnp.float32)
    row8 = lax.broadcasted_iota(jnp.int32, (8, ROWS), 0)

    def stack(values):
        total = jnp.zeros((8, ROWS), jnp.float32)
        for i, value in enumerate(values):
            total = total + jnp.where(row8 == i, value, 0.0)
        return total

    def ranked(values):
        stacked = stack(values)
        ranks = dot(stacked, before)
        counts = jnp.sum(stacked, axis=1, keepdims=True)
        n = len(values)
        return [ranks[i : i + 1] for i in range(n)], [counts[i : i + 1] for i in range(n)]

    def make_orders(m, routes):
        away = (routes[0] // PLANE - y + RING) % RING
        flags = [
            jnp.sum((away == d).astype(jnp.float32), axis=0, keepdims=True) for d in (3, 4, 5)
        ]
        flags = jnp.minimum(dot(stack(flags), order), 1.0)
        p3, f4, m3 = flags[0:1], flags[1:2], flags[2:3]
        fa, fb = f4 * p3 * m3, f4 * p3 * (1.0 - m3)
        fc, fd = f4 * (1.0 - p3) * m3, f4 * (1.0 - p3) * (1.0 - m3)
        (ra, rb, rc, rd, _, _), (na, nb, nc, nd, n3p, n3m) = ranked([fa, fb, fc, fd, p3, m3])
        b_in, c_out = jnp.minimum(nb, LIMIT4), jnp.minimum(nc, LIMIT4)
        b_out, c_in = nb - b_in, nc - c_out
        d_in = jnp.maximum(nd - jnp.minimum(LIMIT3 - n3m - b_out, LIMIT4 - c_out - b_out), 0.0)
        a_in = jnp.minimum(na, LIMIT4 - b_in - c_in - d_in)
        plus4 = (
            jnp.where(ra < a_in, fa, 0.0) + jnp.where(rb < b_in, fb, 0.0)
            + jnp.where(rc < c_out, 0.0, fc) + jnp.where(rd < d_in, fd, 0.0)
        )
        minus4 = f4 - plus4
        plus3, minus3 = p3 * (1.0 - plus4), m3 * (1.0 - minus4)
        groups = [plus4, plus3, 1.0 - plus4 - plus3, minus4, minus3, 1.0 - minus4 - minus3]
        ranks, counts = ranked(groups)
        for way in (PLUS, MINUS):
            g, r, n = (v[3 * way : 3 * way + 3] for v in (groups, ranks, counts))
            spot = g[0] * r[0] + g[1] * (n[0] + r[1]) + g[2] * (n[0] + n[1] + r[2])
            perm[m, way] = (row == spot.astype(jnp.int32)).astype(jnp.bfloat16)
        spot = plus4 * ranks[0] + minus4 * (LIMIT4 + ranks[3]) + (1.0 - f4) * 1024.0
        perm[m, 2] = (row == spot.astype(jnp.int32)).astype(jnp.bfloat16)

    def sort_rows(a, m):
        for way in (PLUS, MINUS):
            for start, size in COLS:
                cols = slice(start, start + size)
                xp[a, way, :, cols] = dot(perm[m, way], x[a, :ROWS, cols]).astype(jnp.bfloat16)

    def remote(source, target, send, receive, device):
        return pltpu.make_async_remote_copy(
            src_ref=source, dst_ref=target, send_sem=send, recv_sem=receive,
            device_id=device, device_id_type=MESH,
        )

    def gather(a, way, hop):
        index = (a * 2 + way) * 4 + hop - 1
        count = HOP_ROWS[hop]
        if hop == 1:
            source = xp.at[a, way]
        else:
            source = x.at[a, pl.ds(place(hop - 1, way) * ROWS, count), :]
        start = FAR * ROWS + HOP_ROWS[4] * way if hop == 4 else place(hop, way) * ROWS
        target = x.at[a, pl.ds(start, count), :]
        return remote(source, target, gs.at[index], gr.at[index], side[way])

    def gather_start(a, hop):
        for way in (PLUS, MINUS):
            gather(a, way, hop).start()

    def gather_wait(a, hop):
        for way in (PLUS, MINUS):
            gather(a, way, hop).wait_recv()

    def relay(a, hop):
        gather_wait(a, hop)
        gather_start(a, hop + 1)

    make_orders(0, fwd_routes)
    for copy in token_loads[FWD]:
        copy.wait()
    sort_rows(FWD, 0)
    pl.semaphore_wait(barrier, len(met))
    gather_start(FWD, 1)

    def piece(owner, i):
        if i < 4:
            return gu.at[owner, pl.ds(448 * i, 448), :]
        return dn.at[owner, pl.ds(128 * (i - 4), 128), :]

    for copy in weight_loads:
        copy.wait()
    to_mate = [remote(piece(seat, i), piece(seat, i), xs.at[i], xr.at[i], mate) for i in range(PIECES)]
    to_twin = [remote(piece(seat, i), piece(seat, i), cs.at[i], cr.at[i], twin) for i in range(PIECES)]
    passed = [
        remote(piece(mate_seat, i), piece(mate_seat, i), rs.at[i], rr.at[i], twin) for i in range(PIECES)
    ]
    for i in range(PIECES):
        to_mate[i].start()
    for i in range(PIECES):
        to_twin[i].start()

    make_orders(1, bwd_routes)
    for a in (SAVED, COT):
        for copy in token_loads[a]:
            copy.wait()
        sort_rows(a, 1)
        gather_start(a, 1)

    expert = lax.broadcasted_iota(jnp.int32, (RING * PLANE, ROWS), 0)
    for m, (routes, mix) in enumerate(((fwd_routes, fwd_mix), (bwd_routes, bwd_mix))):
        spread = jnp.zeros((RING * PLANE, ROWS), jnp.float32)
        for k in range(TOP):
            spread = spread + jnp.where(routes[0, k : k + 1, :] == expert, mix[0, k : k + 1, :], 0.0)
        exact = dict(precision=lax.Precision.HIGHEST, preferred_element_type=jnp.float32)
        natural = jnp.dot(spread, order, **exact)
        for kind in range(4):
            if kind < 3:
                moved = perm[m, kind].astype(jnp.float32)
                value = lax.dot_general(natural, moved, (((1,), (1,)), ((), ())), **exact)
            else:
                value = natural
            for at in range(RING):
                wt[kind, at, pl.ds(4 * m, 4), :] = value[4 * at : 4 * at + 4, :]
        for way in (PLUS, MINUS):
            back[m, way] = perm[m, way].astype(jnp.float32).T.astype(jnp.bfloat16)

    def source_place(delta):
        if delta == 4:
            return FAR
        return place(delta, PLUS) if delta < 4 else place(RING - delta, MINUS)

    mixes = [
        remote(wt.at[(0 if d < 4 else 2 if d == 4 else 1), (y + d) % RING], wr.at[source_place(d)], ws.at[d - 1], wrs.at[d - 1], ring(d))
        for d in range(1, RING)
    ]
    for copy in mixes:
        copy.start()
    wr[OWN] = wt[3, y]

    relay(FWD, 1)
    relay(SAVED, 1)
    relay(COT, 1)
    for copy in mixes:
        copy.wait_recv()
    for s in range(RING):
        wc[pl.ds(s * ROWS, ROWS), :] = wr[s].T
    relay(FWD, 2)
    relay(SAVED, 2)
    relay(COT, 2)
    for i in range(PIECES):
        to_mate[i].wait_recv()
        passed[i].start()
    for i in range(PIECES):
        to_twin[i].wait_recv()
    for i in range(PIECES):
        passed[i].wait_recv()

    def compute_fwd(pair):
        rows = pl.ds(pair * 2 * ROWS, 2 * ROWS)
        for e in range(PLANE):
            projected = dot(x[FWD, rows, :], gu[e])
            gate, up = projected[:, :HID], projected[:, HID:]
            hidden = gate * jax.nn.sigmoid(gate) * up * wc[rows, e : e + 1]
            hid[:, e * HID : (e + 1) * HID] = hidden.astype(jnp.bfloat16)
        for n in range(WIDTH // 256):
            cols = slice(n * 256, (n + 1) * 256)
            total = dot(hid[:, :HID], dn[0, :, cols])
            for e in range(1, PLANE):
                total = total + dot(hid[:, e * HID : (e + 1) * HID], dn[e, :, cols])
            part[0, rows, cols] = total

    def compute_bwd(pair):
        rows = pl.ds(pair * 2 * ROWS, 2 * ROWS)
        for e in range(PLANE):
            projected = dot(x[SAVED, rows, :], gu[e])
            gate, up = projected[:, :HID], projected[:, HID:]
            d_hidden = dot_t(x[COT, rows, :], dn[e]) * wc[rows, 4 + e : 5 + e]
            sig = jax.nn.sigmoid(gate)
            d_gate = d_hidden * up * sig * (1.0 + gate * (1.0 - sig))
            d_up = d_hidden * gate * sig
            both[:, e * 2 * HID : e * 2 * HID + HID] = d_gate.astype(jnp.bfloat16)
            both[:, e * 2 * HID + HID : (e + 1) * 2 * HID] = d_up.astype(jnp.bfloat16)
        for n in range(WIDTH // 256):
            cols = slice(n * 256, (n + 1) * 256)
            total = dot_t(both[:, : 2 * HID], gu[0, cols, :])
            for e in range(1, PLANE):
                total = total + dot_t(both[:, e * 2 * HID : (e + 1) * 2 * HID], gu[e, cols, :])
            part[1, rows, cols] = total

    def back_copy(m, way, step, c):
        index = ((m * 2 + way) * 4 + step - 1) * 4 + c
        start, size = COLS[c]
        cols = pl.ds(start, size)
        count = BACK_ROWS[step]
        if step == 1:
            source = begun.at[m, way, :, cols]
        else:
            source = got.at[m, way, pl.ds(STEP_ROW[step - 1], count), cols]
        target = got.at[m, way, pl.ds(STEP_ROW[step], count), cols]
        return remote(source, target, ss.at[index], sr.at[index], side[1 - way])

    def back_begin(m):
        for c, (start, size) in enumerate(COLS):
            cols = slice(start, start + size)
            for way in (PLUS, MINUS):
                rows = pl.ds(FAR * ROWS + HOP_ROWS[4] * way, HOP_ROWS[4])
                begun[m, way, :, cols] = part[m, rows, cols].astype(jnp.bfloat16)
                back_copy(m, way, 1, c).start()

    def back_step(m, step):
        came, count = BACK_ROWS[step - 1], BACK_ROWS[step]
        for c, (start, size) in enumerate(COLS):
            cols = slice(start, start + size)
            for way in (PLUS, MINUS):
                block = place(5 - step, way) * ROWS
                back_copy(m, way, step - 1, c).wait_recv()
                rows = pl.ds(STEP_ROW[step - 1], came)
                total = got[m, way, rows, cols].astype(jnp.float32) + part[m, pl.ds(block, came), cols]
                got[m, way, rows, cols] = total.astype(jnp.bfloat16)
                if count > came:
                    rest = pl.ds(STEP_ROW[step - 1] + came, count - came)
                    mine = part[m, pl.ds(block + came, count - came), cols]
                    got[m, way, rest, cols] = mine.astype(jnp.bfloat16)
                back_copy(m, way, step, c).start()

    def out_copy(m, c, h):
        start, size = COLS[c]
        index = (m * 4 + c) * 4 + h
        return remote(
            done.at[m, pl.ds(PART * h, PART), pl.ds(start, size)],
            (out_fwd, out_bwd)[m].at[0, :, pl.ds(h * WIDTH + start, size)],
            os_.at[index], or_.at[index], (later, earlier)[m],
        )

    def finish(m):
        for c, (start, size) in enumerate(COLS):
            cols = slice(start, start + size)
            total = part[m, pl.ds(OWN * ROWS, ROWS), cols]
            for way in (PLUS, MINUS):
                back_copy(m, way, 4, c).wait_recv()
                total = total + dot(back[m, way], got[m, way, pl.ds(STEP_ROW[4], ROWS), cols])
            done[m, :, cols] = total.astype(jnp.bfloat16)
            for h in range(4):
                out_copy(m, c, h).start()

    compute_fwd(1)
    relay(FWD, 3)
    compute_fwd(2)
    relay(SAVED, 3)
    compute_fwd(3)
    compute_bwd(1)
    relay(COT, 3)
    gather_wait(FWD, 4)
    compute_fwd(0)
    back_begin(0)
    compute_bwd(2)
    back_step(0, 2)
    compute_bwd(3)
    back_step(0, 3)
    gather_wait(SAVED, 4)
    gather_wait(COT, 4)
    compute_bwd(0)
    back_begin(1)
    back_step(0, 4)
    back_step(1, 2)
    finish(0)
    back_step(1, 3)
    back_step(1, 4)
    finish(1)

    for a in (FWD, SAVED, COT):
        for hop in range(1, 5):
            for way in (PLUS, MINUS):
                gather(a, way, hop).wait_send()
    for i in range(PIECES):
        to_mate[i].wait_send()
        to_twin[i].wait_send()
        passed[i].wait_send()
    for copy in mixes:
        copy.wait_send()
    for m in range(2):
        for c in range(4):
            for step in range(1, 5):
                for way in (PLUS, MINUS):
                    back_copy(m, way, step, c).wait_send()
            for h in range(4):
                out_copy(m, c, h).wait_send()
                out_copy(m, c, h).wait_recv()


def deliver(fwd, bwd, out_fwd, out_bwd):
    out_fwd[...] = fwd[...]
    out_bwd[...] = bwd[...]


def body(fwd_tokens, fwd_routes, fwd_mix, saved, cotangent, bwd_routes, bwd_mix, gate_up, down):
    fwd_routes, fwd_mix, bwd_routes, bwd_mix = (
        jnp.swapaxes(v, 1, 2) for v in (fwd_routes, fwd_mix, bwd_routes, bwd_mix)
    )
    operands = (
        fwd_tokens, fwd_routes, fwd_mix, saved, cotangent, bwd_routes, bwd_mix, gate_up, down
    )
    hbm = pl.BlockSpec(memory_space=pl.ANY)
    vmem = pl.BlockSpec(memory_space=pltpu.VMEM)
    out = jax.ShapeDtypeStruct(operands[0].shape, jnp.bfloat16)
    dma = pltpu.SemaphoreType.DMA
    bf16, f32 = jnp.bfloat16, jnp.float32
    moved = pl.pallas_call(
        kernel,
        out_shape=(out, out),
        in_specs=[hbm, vmem, vmem, hbm, hbm, vmem, vmem, hbm, hbm],
        out_specs=(hbm, hbm),
        scratch_shapes=[
            pltpu.VMEM((3, RING * ROWS, WIDTH), bf16),
            pltpu.VMEM((3, 2, ROWS, WIDTH), bf16),
            pltpu.VMEM((PLANE, WIDTH, 2 * HID), bf16),
            pltpu.VMEM((PLANE, HID, WIDTH), bf16),
            pltpu.VMEM((2, RING * ROWS, WIDTH), f32),
            pltpu.VMEM((2, 2, GOT_ROWS, WIDTH), bf16),
            pltpu.VMEM((2, 2, HOP_ROWS[4], WIDTH), bf16),
            pltpu.VMEM((2, ROWS, WIDTH), bf16),
            pltpu.VMEM((2 * ROWS, PLANE * HID), bf16),
            pltpu.VMEM((2 * ROWS, PLANE * 2 * HID), bf16),
            pltpu.VMEM((2, 3, ROWS, ROWS), bf16),
            pltpu.VMEM((2, 2, ROWS, ROWS), bf16),
            pltpu.VMEM((4, RING, 8, ROWS), f32),
            pltpu.VMEM((RING, 8, ROWS), f32),
            pltpu.VMEM((RING * ROWS, 8), f32),
            dma((14,)),
            dma((24,)), dma((24,)),
            dma((64,)), dma((64,)),
            dma((32,)), dma((32,)),
            dma((PIECES,)), dma((PIECES,)),
            dma((PIECES,)), dma((PIECES,)),
            dma((PIECES,)), dma((PIECES,)),
            dma((RING - 1,)), dma((RING - 1,)),
        ],
        name="moe_relay",
        compiler_params=pltpu.CompilerParams(
            collective_id=0, has_side_effects=True, vmem_limit_bytes=60 * 1024 * 1024
        ),
    )(*operands)
    return pl.pallas_call(
        deliver,
        out_shape=(out, out),
        in_specs=[vmem, vmem],
        out_specs=(vmem, vmem),
        name="deliver",
    )(*moved)


def solution(mesh):
    spec3 = P("pipe", "expert", None)
    spec4 = P("pipe", "expert", None, None)
    return jax.shard_map(
        body,
        mesh=mesh,
        in_specs=(spec3,) * 7 + (spec4,) * 2,
        out_specs=(spec3, spec3),
        check_vma=False,
    )
```

time: 208 us -> 185 us (0.89)
  Pallas kernels: 198 us -> 184 us
  local copies, waits for them, and re-layouts: 9.3 us -> 0 us
    pallas_call x1, Pallas kernels: 198 us -> 182 us  [body(): pl.pallas_call(kernel, out_shape=(out, out), in_specs=[hbm, vmem, vmem, h...]
    unnamed x6 -> x0, local copies, waits for them, and re-layouts: 9.3 us -> none
    pallas_call x0 -> x1, Pallas kernels: none -> 2.11 us  [body(): pl.pallas_call(deliver, out_shape=(out, out), in_specs=[vmem, vmem], out_...]
where the time goes in v2:
time: 185 us; the launch traced here: 184 us
  Pallas kernels  184 us (99%)
    pallas_call x1, Pallas kernels, body(): pl.pallas_call(kernel, out_shape=(out, out), in_specs=[hbm, vmem, vmem, h...  182 us

profile of v2, /device:TPU:24, one launch (start us, length us, event | category | flops | bytes accessed | tf_op | source)
XLA Modules:
  0.0 184.4 jit_solution(4672896786376834587)
XLA Ops:
  0.6 181.6 %moe_relay.1 = (bf16[1,32,7168]{2,1,0:T(8,128)(2,1)}, bf16[1,32,7168]{2,1,0:T(8,128)(2,1)}) custom-call(bf16[1,32,7168]{2,1,0:T(8,128)(2,1)} %fwd_tokens.1, s32[1,4,128]{2,1,0:T(4,128)} %bitcast.4, f32[1,4,128]{2,1,0:T(4,128)} %bitcast.5, bf16[1,32,7168]{2,1,0:T(8,128)(2,1)} %saved.1, bf16[1,32,7168]{2,1,0:T(8,128)(2,1)} %cotangent.1, s32[1,4,128]{2,1,0:T(4,128)} %bitcast.6, ...), custom_call_target="tpu_custom_call" | custom-call | tf_op jit(solution)/shard_map/moe_relay/pallas_call | solution.py:400
  182.3 2.1 %deliver.1 = (bf16[1,32,7168]{2,1,0:T(8,128)(2,1)}, bf16[1,32,7168]{2,1,0:T(8,128)(2,1)}) custom-call(bf16[1,32,7168]{2,1,0:T(8,128)(2,1)} %get-tuple-element.4.fwd, bf16[1,32,7168]{2,1,0:T(8,128)(2,1)} %get-tuple-element.5.bwd), custom_call_target="tpu_custom_call" | custom-call | tf_op jit(solution)/shard_map/deliver/pallas_call | solution.py:435

commit v3 on v2

--- a/solution.py
+++ b/solution.py
@@ -46,7 +46,7 @@
     fwd_tokens, fwd_routes, fwd_mix, saved, cotangent, bwd_routes, bwd_mix, gate_up, down,
     out_fwd, out_bwd,
     x, xp, gu, dn, part, got, begun, done, hid, both, perm, back, wt, wr, wc,
-    load_sem, gs, gr, ss, sr, os_, or_, xs, xr, cs, cr, rs, rr, ws, wrs,
+    load_sem, gs, gr, ss, sr, os_, or_, xs, xr, cs, cr, rs, rr, ws, wrs, twin_here, pipe_here,
 ):
     ex = lax.axis_index("expert")
     pi = lax.axis_index("pipe")
@@ -66,6 +66,21 @@
     earlier = {"pipe": (pi + sections - 1) % sections, "expert": ex}
     side = {PLUS: ring(1), MINUS: ring(RING - 1)}
 
+    barrier = pltpu.get_barrier_semaphore()
+    odd = pi % 2
+    met = [ring(d) for d in range(1, RING)] + [mate]
+    for device in met:
+        pl.semaphore_signal(barrier, inc=1, device_id=device, device_id_type=MESH)
+
+    @pl.when(core == 1)
+    def _():
+        pl.semaphore_signal(barrier, inc=1, device_id=twin, device_id_type=MESH)
+
+    @pl.when(odd == 0)
+    def _():
+        pl.semaphore_signal(barrier, inc=1, device_id=later, device_id_type=MESH)
+        pl.semaphore_signal(barrier, inc=1, device_id=earlier, device_id_type=MESH)
+
     def load(index, source, target):
         copy = pltpu.make_async_copy(source, target, load_sem.at[index])
         copy.start()
@@ -78,11 +93,6 @@
             for h in range(4)
         ])
     weight_loads = [load(12, gate_up.at[0, 0], gu.at[seat]), load(13, down.at[0, 0], dn.at[seat])]
-
-    barrier = pltpu.get_barrier_semaphore()
-    met = [ring(d) for d in range(1, RING)] + [mate, twin, later, earlier]
-    for device in met:
-        pl.semaphore_signal(barrier, inc=1, device_id=device, device_id_type=MESH)
 
     lane = lax.broadcasted_iota(jnp.int32, (ROWS, ROWS), 1)
     row = lax.broadcasted_iota(jnp.int32, (ROWS, ROWS), 0)
@@ -171,7 +181,17 @@
     for copy in token_loads[FWD]:
         copy.wait()
     sort_rows(FWD, 0)
-    pl.semaphore_wait(barrier, len(met))
+    pl.semaphore_wait(barrier, len(met) + 1 - core + 2 * odd)
+
+    @pl.when(odd == 1)
+    def _():
+        pl.semaphore_signal(pipe_here, inc=1, device_id=later, device_id_type=MESH)
+        pl.semaphore_signal(pipe_here, inc=1, device_id=earlier, device_id_type=MESH)
+
+    @pl.when(core == 0)
+    def _():
+        pl.semaphore_signal(twin_here, inc=1, device_id=twin, device_id_type=MESH)
+
     gather_start(FWD, 1)
 
     def piece(owner, i):
@@ -188,8 +208,6 @@
     ]
     for i in range(PIECES):
         to_mate[i].start()
-    for i in range(PIECES):
-        to_twin[i].start()
 
     make_orders(1, bwd_routes)
     for a in (SAVED, COT):
@@ -228,6 +246,13 @@
     for copy in mixes:
         copy.start()
     wr[OWN] = wt[3, y]
+
+    @pl.when(core == 1)
+    def _():
+        pl.semaphore_wait(twin_here, 1)
+
+    for i in range(PIECES):
+        to_twin[i].start()
 
     relay(FWD, 1)
     relay(SAVED, 1)
@@ -355,6 +380,11 @@
     back_begin(1)
     back_step(0, 4)
     back_step(1, 2)
+
+    @pl.when(odd == 0)
+    def _():
+        pl.semaphore_wait(pipe_here, 2)
+
     finish(0)
     back_step(1, 3)
     back_step(1, 4)
@@ -426,6 +456,8 @@
             dma((PIECES,)), dma((PIECES,)),
             dma((PIECES,)), dma((PIECES,)),
             dma((RING - 1,)), dma((RING - 1,)),
+            pltpu.SemaphoreType.REGULAR,
+            pltpu.SemaphoreType.REGULAR,
         ],
         name="moe_relay",
         compiler_params=pltpu.CompilerParams(

time: 185 us -> 182 us (0.984)
  the two profiles are of different devices: /device:TPU:24 before, /device:TPU:198 now
where the time goes in v3:
time: 182 us
  Pallas kernels  182 us (100%)
    pallas_call x1, Pallas kernels, body(): pl.pallas_call(kernel, out_shape=(out, out), in_specs=[hbm, vmem, vmem, h...  179 us

profile of v3, /device:TPU:198, one launch (start us, length us, event | category | flops | bytes accessed | tf_op | source)
XLA Modules:
  0.0 182.2 jit_solution(11143872036407660551)
XLA Ops:
  0.6 179.5 %moe_relay.1 = (bf16[1,32,7168]{2,1,0:T(8,128)(2,1)}, bf16[1,32,7168]{2,1,0:T(8,128)(2,1)}) custom-call(bf16[1,32,7168]{2,1,0:T(8,128)(2,1)} %fwd_tokens.1, s32[1,4,128]{2,1,0:T(4,128)} %bitcast.4, f32[1,4,128]{2,1,0:T(4,128)} %bitcast.5, bf16[1,32,7168]{2,1,0:T(8,128)(2,1)} %saved.1, bf16[1,32,7168]{2,1,0:T(8,128)(2,1)} %cotangent.1, s32[1,4,128]{2,1,0:T(4,128)} %bitcast.6, ...), custom_call_target="tpu_custom_call" | custom-call | tf_op jit(solution)/shard_map/moe_relay/pallas_call | solution.py:430
  180.1 2.1 %deliver.1 = (bf16[1,32,7168]{2,1,0:T(8,128)(2,1)}, bf16[1,32,7168]{2,1,0:T(8,128)(2,1)}) custom-call(bf16[1,32,7168]{2,1,0:T(8,128)(2,1)} %get-tuple-element.4.fwd, bf16[1,32,7168]{2,1,0:T(8,128)(2,1)} %get-tuple-element.5.bwd), custom_call_target="tpu_custom_call" | custom-call | tf_op jit(solution)/shard_map/deliver/pallas_call | solution.py:467
